TPU v7x, 32 devices: a whole 2x2x4 slice. The times are simulated.
32 devices in a mesh: frame: 8 (over z, y), tensor: 2 (over x), dp: 2 (over core).
Axes of the slice: x: 2, y: 2, z: 4, core: 2. Of those that a mesh axis runs over, the one named last changes fastest.
Arguments:
- q_proj: bfloat16 [8192, 768], P(('dp', 'frame'), 'tensor'), parts along dimension 0
- k_proj: bfloat16 [8192, 768], P(('dp', 'frame'), 'tensor'), parts along dimension 0
- v_proj: bfloat16 [8192, 768], P(('dp', 'frame'), 'tensor'), parts along dimension 0, may hold values from -6 to 6
- gain_q: float32 [768], P('tensor'), may hold values from 0.5 to 6
- gain_k: float32 [768], P('tensor'), may hold values from 0.5 to 6
- tiles: int32 [64, 12], P('dp'), parts along dimension 0, may hold values from 0 to 31, as said below
Outputs:
- attended: bfloat16 [8192, 768], P(('dp', 'frame'), 'tensor'), parts along dimension 0
There are 2 independent parts, one for each index of `dp`. A program takes and returns all parts, laid end to end along the dimension named above; an argument that names none is the same for every part. Nothing has to cross between parts.
Inputs may be any that keep to these rules, and one draw needn't show every extreme that they name: `tiles`: row q lists 12 distinct key blocks: q first; then 8 blocks whose slab (group of 4 consecutive blocks, one frame slab) is at most 2 slabs from the slab of q; then 3 blocks that are each the first block of a slab more than 2 slabs away. Farther groups are listed less often.
All inputs are finite; a program needn't handle non-finite values.
Results may differ from a plain program's by a relative error of at most 0.007.
The roundings to bfloat16 on the way count: a program that leaves them out, or rounds other values in their place, can miss the bound.
Values may be sent and summed in bfloat16 or wider, within the bound.
A program may use at most 128 MiB of HBM per device.

v0:
```python
import math

import jax
import jax.numpy as jnp
from jax import lax
from jax.sharding import PartitionSpec as P

HD = 128
BLK = 128


EPS = 1e-06


def attend(state_now, q_heads, keys, values, key_ids, q_tiles):
    run_max, run_sum, run_acc = state_now
    head_count = run_max.shape[0]
    tok_rows = q_heads.shape[0]
    length = keys.shape[0]
    k_heads = keys.reshape(length, head_count, HD)
    v_heads = values.reshape(length, head_count, HD)
    scores = jnp.einsum("qhd,khd->hqk", q_heads, k_heads, preferred_element_type=jnp.float32) * (
        1.0 / math.sqrt(HD)
    )
    listed = jnp.any(q_tiles[:, :, None] == key_ids[None, None, :], axis=1)
    listed = jnp.repeat(listed, tok_rows // q_tiles.shape[0], axis=0)[None]
    scores = jnp.where(listed, scores, -1e30)
    new_max = jnp.maximum(run_max, jnp.max(scores, axis=-1))
    factor = jnp.exp(run_max - new_max)
    weights = jnp.where(listed, jnp.exp(scores - new_max[..., None]), 0.0)
    new_sum = run_sum * factor + jnp.sum(weights, axis=-1)
    product = jnp.einsum(
        "hqk,khd->hqd", weights.astype(jnp.bfloat16), v_heads, preferred_element_type=jnp.float32
    )
    new_acc = run_acc * factor[..., None] + product
    return (new_max, new_sum, new_acc)


def sweep(state_now, q_heads, keys, values, key_ids, q_tiles):
    length = keys.shape[0]
    sub_rows = math.gcd(length, 512)
    steps_count = length // sub_rows
    width = keys.shape[1]
    inputs = (
        keys.reshape(steps_count, sub_rows, width),
        values.reshape(steps_count, sub_rows, width),
        key_ids.reshape(steps_count, sub_rows),
    )

    def one_step(carried, parts_now):
        return (attend(carried, q_heads, parts_now[0], parts_now[1], parts_now[2], q_tiles), None)

    final_state, unused = lax.scan(one_step, state_now, inputs)
    return final_state


def body(q_proj, k_proj, v_proj, gain_q, gain_k, tiles):
    tok_rows, width = q_proj.shape
    head_count = width // HD
    q_wide = q_proj.astype(jnp.float32)
    k_wide = k_proj.astype(jnp.float32)
    row_sums = lax.psum(
        (jnp.sum(q_wide * q_wide, axis=1), jnp.sum(k_wide * k_wide, axis=1)), "tensor"
    )
    full_width = width * lax.axis_size("tensor")
    q_norm = (q_wide * lax.rsqrt(row_sums[0] / full_width + EPS)[:, None] * gain_q).astype(
        jnp.bfloat16
    )
    k_norm = (k_wide * lax.rsqrt(row_sums[1] / full_width + EPS)[:, None] * gain_k).astype(
        jnp.bfloat16
    )
    blocks = tok_rows // BLK
    frame_pos = lax.axis_index("frame")
    q_tiles = lax.dynamic_slice_in_dim(tiles, frame_pos * blocks, blocks, 0)
    q_heads = q_norm.reshape(tok_rows, head_count, HD)
    kv_pair = jnp.stack([k_norm, v_proj])
    state_now = (
        jnp.full((head_count, tok_rows), -1e30, jnp.float32),
        jnp.zeros((head_count, tok_rows), jnp.float32),
        jnp.zeros((head_count, tok_rows, HD), jnp.float32),
    )
    portion = lax.all_gather(kv_pair, "frame", axis=1, tiled=True)
    length = portion.shape[1]
    key_ids = jnp.arange(length, dtype=jnp.int32) // BLK
    state_now = sweep(state_now, q_heads, portion[0], portion[1], key_ids, q_tiles)
    run_max, run_sum, run_acc = state_now
    result = run_acc / run_sum[..., None]
    return jnp.transpose(result, (1, 0, 2)).reshape(tok_rows, width).astype(jnp.bfloat16)


def solution(mesh):
    return jax.shard_map(
        body,
        mesh=mesh,
        in_specs=(
            P(("dp", "frame"), "tensor"),
            P(("dp", "frame"), "tensor"),
            P(("dp", "frame"), "tensor"),
            P("tensor"),
            P("tensor"),
            P("dp", None),
        ),
        out_specs=P(("dp", "frame"), "tensor"),
        check_vma=False,
    )
```

profile of v0, /device:TPU:4, one launch (start us, length us, event | category | flops | bytes accessed | tf_op | source)
XLA Modules:
  0.0 237.1 jit_solution(421295058111240302)
XLA Ops:
  9.0 4.9 %all-reduce = (f32[512]{0:T(512)S(1)}, f32[512]{0:T(512)S(1)}) all-reduce(f32[512]{0:T(512)S(1)} %fusion.13, f32[512]{0:T(512)S(1)} %fusion.16), channel_id=1, replica_groups=mesh['frame'=8,'tensor'=2,'dp'=2] {'tensor'}, use_global_device_ids=true, to_apply=%region_1.0 | all-reduce | flops 1024 | bytes 8192 | tf_op jit(solution)/shard_map/psum | solution.py:62
  15.1 2.0 pad_maximum_fusion
  18.3 98.3 %all-gather.2.cloned.1.call-done = bf16[2,4096,384]{2,1,0:T(8,128)(2,1)} async-done(((bf16[2,512,384]{2,1,0:T(8,128)(2,1)}), bf16[2,4096,384]{2,1,0:T(8,128)(2,1)}) %all-gather.2.cloned.1.call-update) | async-done | bytes 6291472 | tf_op jit(solution)/shard_map/all_gather | solution.py:82
  116.6 6.1 %fusion.23 = (bf16[1,4096,384]{2,1,0:T(8,128)(2,1)}, bf16[1,4096,384]{2,1,0:T(8,128)(2,1)}) fusion(bf16[2,4096,384]{2,1,0:T(8,128)(2,1)} %all-gather.2.cloned.1.call-done), kind=kLoop, calls=%fused_computation.46 | loop fusion | bytes 12582912 | tf_op jit(solution)/shard_map/slice | solution.py:85
  122.7 105.1 %while.15 = (s32[]{:T(128)}, f32[3,512]{1,0:T(4,128)S(1)}, f32[3,512]{1,0:T(4,128)S(1)}, f32[3,512,128]{2,1,0:T(8,128)}, s32[4,12]{0,1:T(8,128)S(1)}, /*index=5*...) while((s32[]{:T(128)}, f32[3,512]{1,0:T(4,128)S(1)}, ...), condition=%wide.region_8.9_spmd.clone, body=%wide.region_4.8_spmd.clone.sunk | while | flops 413521408 | bytes 17021248 | solution.py:53
  124.8 1.9 constant_dynamic-slice_fusion.7
  127.7 2.0 fusion.39
  130.5 1.9 copy.53
  132.4 3.2 %fusion.42 = f32[3,512,128]{2,1,0:T(8,128)} fusion(bf16[512,3,128]{0,2,1:T(8,128)(2,1)} %bitcast.61, f32[3,512,512]{2,1,0:T(8,128)S(1)} %get-tuple-element.205, f32[3,512]{1,0:T(4,128)S(1)} %select_maximum_fusion.2, pred[512,512]{0,1:T(8,128)(4,1)S(1)} %bitcast.58, f32[3,512,128]{2,1,0:T(8,128)} %get-tuple-element.223, ...), kind=kOutput, calls=%fused_computation.7.clone.1 | convolution fusion | flops 205848576 | bytes 5386241 | tf_op jit(solution)/shard_map/while/body/eval_jaxpr/hqk,khd->hqd/dot_general | solution.py:32
  137.7 1.9 constant_dynamic-slice_fusion.7
  140.6 2.0 fusion.39
  143.4 1.9 copy.53
  145.3 3.5 %fusion.42 = f32[3,512,128]{2,1,0:T(8,128)} fusion(bf16[512,3,128]{0,2,1:T(8,128)(2,1)} %bitcast.61, f32[3,512,512]{2,1,0:T(8,128)S(1)} %get-tuple-element.205, f32[3,512]{1,0:T(4,128)S(1)} %select_maximum_fusion.2, pred[512,512]{0,1:T(8,128)(4,1)S(1)} %bitcast.58, f32[3,512,128]{2,1,0:T(8,128)} %get-tuple-element.223, ...), kind=kOutput, calls=%fused_computation.7.clone.1 | convolution fusion | flops 205848576 | bytes 5386241 | tf_op jit(solution)/shard_map/while/body/eval_jaxpr/hqk,khd->hqd/dot_general | solution.py:32
  150.9 1.9 constant_dynamic-slice_fusion.7
  153.7 2.0 fusion.39
  156.6 1.9 copy.53
  158.5 3.5 %fusion.42 = f32[3,512,128]{2,1,0:T(8,128)} fusion(bf16[512,3,128]{0,2,1:T(8,128)(2,1)} %bitcast.61, f32[3,512,512]{2,1,0:T(8,128)S(1)} %get-tuple-element.205, f32[3,512]{1,0:T(4,128)S(1)} %select_maximum_fusion.2, pred[512,512]{0,1:T(8,128)(4,1)S(1)} %bitcast.58, f32[3,512,128]{2,1,0:T(8,128)} %get-tuple-element.223, ...), kind=kOutput, calls=%fused_computation.7.clone.1 | convolution fusion | flops 205848576 | bytes 5386241 | tf_op jit(solution)/shard_map/while/body/eval_jaxpr/hqk,khd->hqd/dot_general | solution.py:32
  164.0 1.9 constant_dynamic-slice_fusion.7
  166.9 2.0 fusion.39
  171.7 3.5 %fusion.42 = f32[3,512,128]{2,1,0:T(8,128)} fusion(bf16[512,3,128]{0,2,1:T(8,128)(2,1)} %bitcast.61, f32[3,512,512]{2,1,0:T(8,128)S(1)} %get-tuple-element.205, f32[3,512]{1,0:T(4,128)S(1)} %select_maximum_fusion.2, pred[512,512]{0,1:T(8,128)(4,1)S(1)} %bitcast.58, f32[3,512,128]{2,1,0:T(8,128)} %get-tuple-element.223, ...), kind=kOutput, calls=%fused_computation.7.clone.1 | convolution fusion | flops 205848576 | bytes 5386241 | tf_op jit(solution)/shard_map/while/body/eval_jaxpr/hqk,khd->hqd/dot_general | solution.py:32
  177.2 1.9 constant_dynamic-slice_fusion.7
  180.1 2.0 fusion.39
  184.8 3.5 %fusion.42 = f32[3,512,128]{2,1,0:T(8,128)} fusion(bf16[512,3,128]{0,2,1:T(8,128)(2,1)} %bitcast.61, f32[3,512,512]{2,1,0:T(8,128)S(1)} %get-tuple-element.205, f32[3,512]{1,0:T(4,128)S(1)} %select_maximum_fusion.2, pred[512,512]{0,1:T(8,128)(4,1)S(1)} %bitcast.58, f32[3,512,128]{2,1,0:T(8,128)} %get-tuple-element.223, ...), kind=kOutput, calls=%fused_computation.7.clone.1 | convolution fusion | flops 205848576 | bytes 5386241 | tf_op jit(solution)/shard_map/while/body/eval_jaxpr/hqk,khd->hqd/dot_general | solution.py:32
  190.4 1.9 constant_dynamic-slice_fusion.7
  193.2 2.0 fusion.39
  198.0 3.5 %fusion.42 = f32[3,512,128]{2,1,0:T(8,128)} fusion(bf16[512,3,128]{0,2,1:T(8,128)(2,1)} %bitcast.61, f32[3,512,512]{2,1,0:T(8,128)S(1)} %get-tuple-element.205, f32[3,512]{1,0:T(4,128)S(1)} %select_maximum_fusion.2, pred[512,512]{0,1:T(8,128)(4,1)S(1)} %bitcast.58, f32[3,512,128]{2,1,0:T(8,128)} %get-tuple-element.223, ...), kind=kOutput, calls=%fused_computation.7.clone.1 | convolution fusion | flops 205848576 | bytes 5386241 | tf_op jit(solution)/shard_map/while/body/eval_jaxpr/hqk,khd->hqd/dot_general | solution.py:32
  203.5 1.9 constant_dynamic-slice_fusion.7
  206.4 2.0 fusion.39
  211.1 3.5 %fusion.42 = f32[3,512,128]{2,1,0:T(8,128)} fusion(bf16[512,3,128]{0,2,1:T(8,128)(2,1)} %bitcast.61, f32[3,512,512]{2,1,0:T(8,128)S(1)} %get-tuple-element.205, f32[3,512]{1,0:T(4,128)S(1)} %select_maximum_fusion.2, pred[512,512]{0,1:T(8,128)(4,1)S(1)} %bitcast.58, f32[3,512,128]{2,1,0:T(8,128)} %get-tuple-element.223, ...), kind=kOutput, calls=%fused_computation.7.clone.1 | convolution fusion | flops 205848576 | bytes 5386241 | tf_op jit(solution)/shard_map/while/body/eval_jaxpr/hqk,khd->hqd/dot_general | solution.py:32
  216.7 1.9 constant_dynamic-slice_fusion.7
  219.6 2.0 fusion.39
  224.3 3.5 %fusion.42 = f32[3,512,128]{2,1,0:T(8,128)} fusion(bf16[512,3,128]{0,2,1:T(8,128)(2,1)} %bitcast.61, f32[3,512,512]{2,1,0:T(8,128)S(1)} %get-tuple-element.205, f32[3,512]{1,0:T(4,128)S(1)} %select_maximum_fusion.2, pred[512,512]{0,1:T(8,128)(4,1)S(1)} %bitcast.58, f32[3,512,128]{2,1,0:T(8,128)} %get-tuple-element.223, ...), kind=kOutput, calls=%fused_computation.7.clone.1 | convolution fusion | flops 205848576 | bytes 5386241 | tf_op jit(solution)/shard_map/while/body/eval_jaxpr/hqk,khd->hqd/dot_general | solution.py:32
  (106 shorter events, 47.3 us)
Async XLA Ops:
  6.5 11.7 %copy-start = (s32[32,12]{0,1:T(8,128)S(1)}, s32[32,12]{0,1:T(8,128)}, u32[]{:S(2)}) copy-start(s32[32,12]{0,1:T(8,128)} %param.13) | copy-start | bytes 4612
  6.5 10.6 %copy-start.1 = (f32[384]{0:T(512)S(1)}, f32[384]{0:T(512)}, u32[]{:S(2)}) copy-start(f32[384]{0:T(512)} %param.11) | copy-start | bytes 4612
  6.5 110.1 %all-gather.2.cloned.1.call-start = ((), (), s32[]{:S(2)}) async-start(), calls=%async_computation | async-start | bytes 7077888 | tf_op jit(solution)/shard_map/all_gather | solution.py:82
Sparse Core Ops, SparseCore 0:
  17.2 99.3 all-gather.1
where the time goes:
time: 241 us; the launch traced here: 237 us
  waiting for transfers between devices  98.3 us (41%)
  local copies, waits for them, and re-layouts  64.5 us (27%)
  matrix products  43.3 us (18%)
  between operations  13.5 us (6%)
  other arithmetic  12.1 us (5%)
  blocking collectives  4.94 us (2%)
    all_gather x1, waiting for transfers between devices, body(): portion = lax.all_gather(kv_pair, 'frame', axis=1, tiled=True)  98.3 us
    dynamic_slice x32, local copies, waits for them, and re-layouts, sweep(): final_state, unused = lax.scan(one_step, state_now, inputs)  38.4 us
    dot_general x8, matrix products, attend(): jnp.einsum('hqk,khd->hqd', weights.astype(jnp.bfloat16), v_heads, preferr...  27.6 us
    dot_general x8, matrix products, attend(): jnp.einsum('qhd,khd->hqk', q_heads, k_heads, preferred_element_type=jnp.f...  15.7 us
    broadcast_in_dim x8, local copies, waits for them, and re-layouts, attend(): listed = jnp.repeat(listed, tok_rows // q_tiles.shape[0], axis=0)[None]  12.8 us
    reduce_sum x8, other arithmetic, attend(): new_sum = run_sum * factor + jnp.sum(weights, axis=-1)  6.45 us
    slice x1, local copies, waits for them, and re-layouts, body(): portion[1]  6.13 us
    psum x1, blocking collectives, body(): lax.psum((jnp.sum(q_wide * q_wide, axis=1), jnp.sum(k_wide * k_wide, axis...  4.94 us
  transfers between devices with their start and end apart: 1, of which 1 were waited for; matrix products, arithmetic and copies ran while one was open for 0% of the time, Pallas kernels for 0%

commit v1 on v0

v1 whole, which is shorter than its diff:
```python
import functools
import math

import jax
import jax.numpy as jnp
from jax import lax
from jax.experimental import pallas as pl
from jax.experimental.pallas import tpu as pltpu
from jax.sharding import PartitionSpec as P

HD = 128
BLK = 128
NEAR = 2
EPS = 1e-06
MASKED = -1e30
MESH = pl.DeviceIdType.MESH


def kernel(
    frames,
    tensors,
    tiles_ref,
    q_ref,
    k_ref,
    v_ref,
    gq_ref,
    gk_ref,
    out_ref,
    kbuf,
    vbuf,
    qn,
    sums,
    listed,
    acc_ref,
    max_ref,
    sum_ref,
    send_k,
    send_v,
    recv_k,
    recv_v,
    send_s,
    recv_s,
):
    me = lax.axis_index("frame")
    tpos = lax.axis_index("tensor")
    rows, width = q_ref.shape
    heads = width // HD
    blocks = rows // BLK
    slots = tiles_ref.shape[1]

    barrier = pltpu.get_barrier_semaphore()
    for step in range(1, frames):
        pl.semaphore_signal(
            barrier, inc=1, device_id={"frame": lax.rem(me + step, frames)}, device_id_type=MESH
        )
    for step in range(1, tensors):
        pl.semaphore_signal(
            barrier, inc=1, device_id={"tensor": lax.rem(tpos + step, tensors)}, device_id_type=MESH
        )
    pl.semaphore_wait(barrier, frames - 1 + tensors - 1)

    def full_copy(src, buf, send, recv, dest):
        return pltpu.make_async_remote_copy(
            src_ref=src,
            dst_ref=buf.at[me],
            send_sem=send.at[dest],
            recv_sem=recv.at[me],
            device_id={"frame": dest},
            device_id_type=MESH,
        )

    def first_copy(src, buf, send, recv, dest):
        return pltpu.make_async_remote_copy(
            src_ref=src.at[pl.ds(0, BLK)],
            dst_ref=buf.at[me, pl.ds(0, BLK)],
            send_sem=send.at[dest],
            recv_sem=recv.at[me],
            device_id={"frame": dest},
            device_id_type=MESH,
        )

    side = 1 - 2 * lax.rem(me, 2)
    order = (me + side, me + 2, me - 2, me - side)

    def each_near(action):
        for other in order:

            @pl.when(jnp.logical_and(other >= 0, other < frames))
            def _():
                action(other)

    def each_far(action):
        @pl.loop(0, frames)
        def _(other):
            @pl.when(jnp.abs(other - me) > NEAR)
            def _():
                action(other)

    each_near(lambda dest: full_copy(v_ref, vbuf, send_v, recv_v, dest).start())

    def squares(ref):
        total = None
        for head in range(heads):
            wide = ref[:, head * HD : (head + 1) * HD].astype(jnp.float32)
            total = wide * wide if total is None else total + wide * wide
        return jnp.sum(jnp.transpose(total), axis=0, keepdims=True)

    sums[tpos] = jnp.concatenate(
        [squares(q_ref), squares(k_ref), jnp.zeros((6, rows), jnp.float32)], axis=0
    )

    def sums_copy(peer):
        return pltpu.make_async_remote_copy(
            src_ref=sums.at[tpos],
            dst_ref=sums.at[tpos],
            send_sem=send_s.at[peer],
            recv_sem=recv_s.at[tpos],
            device_id={"tensor": peer},
            device_id_type=MESH,
        )

    for step in range(1, tensors):
        sums_copy(lax.rem(tpos + step, tensors)).start()

    each_far(lambda dest: first_copy(v_ref, vbuf, send_v, recv_v, dest).start())

    for slot in range(slots):
        listed[slot : slot + 1, :] = jnp.concatenate(
            [
                jnp.full((1, BLK), tiles_ref[me * blocks + block, slot], jnp.int32)
                for block in range(blocks)
            ],
            axis=1,
        )

    for step in range(1, tensors):
        peer = lax.rem(tpos + step, tensors)
        pltpu.make_async_copy(sums.at[peer], sums.at[peer], recv_s.at[peer]).wait()
    total = sums[0]
    for other in range(1, tensors):
        total = total + sums[other]
    factor = lax.rsqrt(total / (width * tensors) + EPS)

    def normed(ref, row, gain, store):
        scale = jnp.transpose(jnp.broadcast_to(factor[row : row + 1], (HD, rows)))
        for head in range(heads):
            columns = slice(head * HD, (head + 1) * HD)
            wide = ref[:, columns].astype(jnp.float32)
            store(columns, (wide * scale * gain[:, columns]).astype(jnp.bfloat16))

    def store_k(columns, value):
        kbuf[me, :, columns] = value

    def store_q(columns, value):
        qn[:, columns] = value

    normed(k_ref, 1, gk_ref, store_k)
    each_near(lambda dest: full_copy(kbuf.at[me], kbuf, send_k, recv_k, dest).start())
    each_far(lambda dest: first_copy(kbuf.at[me], kbuf, send_k, recv_k, dest).start())
    normed(q_ref, 0, gq_ref, store_q)

    acc_ref[...] = jnp.zeros_like(acc_ref)
    max_ref[...] = jnp.full_like(max_ref, MASKED)
    sum_ref[...] = jnp.zeros_like(sum_ref)
    to_exponent = math.log2(math.e) / math.sqrt(HD)

    def attend(slab, keys, values):
        count = keys.shape[0] // BLK
        biases = []
        for block in range(count):
            hit = jnp.any(listed[0:slots, :] == slab * blocks + block, axis=0, keepdims=True)
            biases.append(jnp.where(hit, 0.0, MASKED))
        for head in range(heads):
            columns = slice(head * HD, (head + 1) * HD)
            scores = lax.dot_general(
                keys[:, columns],
                qn[:, columns],
                (((1,), (1,)), ((), ())),
                preferred_element_type=jnp.float32,
            )
            parts = [
                scores[block * BLK : (block + 1) * BLK] * to_exponent + biases[block]
                for block in range(count)
            ]
            top = functools.reduce(jnp.maximum, parts)
            old_max = max_ref[head : head + 1, :]
            new_max = jnp.maximum(old_max, jnp.max(top, axis=0, keepdims=True))
            shrink = jnp.exp2(old_max - new_max)
            weights = [jnp.exp2(part - new_max) for part in parts]
            added = functools.reduce(jnp.add, weights)
            max_ref[head : head + 1, :] = new_max
            sum_ref[head : head + 1, :] = sum_ref[head : head + 1, :] * shrink + jnp.sum(
                added, axis=0, keepdims=True
            )
            rounded = jnp.concatenate([weight.astype(jnp.bfloat16) for weight in weights], axis=0)
            product = lax.dot_general(
                values[:, columns],
                rounded,
                (((0,), (0,)), ((), ())),
                preferred_element_type=jnp.float32,
            )
            acc_ref[head] = acc_ref[head] * shrink + product

    attend(me, kbuf.at[me], v_ref)

    def near_step(other):
        pltpu.make_async_copy(vbuf.at[other], vbuf.at[other], recv_v.at[other]).wait()
        pltpu.make_async_copy(kbuf.at[other], kbuf.at[other], recv_k.at[other]).wait()
        attend(other, kbuf.at[other], vbuf.at[other])

    each_near(near_step)

    def far_step(other):
        piece_v = vbuf.at[other, pl.ds(0, BLK)]
        piece_k = kbuf.at[other, pl.ds(0, BLK)]
        pltpu.make_async_copy(piece_v, piece_v, recv_v.at[other]).wait()
        pltpu.make_async_copy(piece_k, piece_k, recv_k.at[other]).wait()
        attend(other, piece_k, piece_v)

    each_far(far_step)

    for head in range(heads):
        value = acc_ref[head] / sum_ref[head : head + 1, :]
        out_ref[:, head * HD : (head + 1) * HD] = jnp.transpose(value).astype(jnp.bfloat16)

    each_near(lambda dest: full_copy(v_ref, vbuf, send_v, recv_v, dest).wait_send())
    each_near(lambda dest: full_copy(kbuf.at[me], kbuf, send_k, recv_k, dest).wait_send())
    each_far(lambda dest: first_copy(v_ref, vbuf, send_v, recv_v, dest).wait_send())
    each_far(lambda dest: first_copy(kbuf.at[me], kbuf, send_k, recv_k, dest).wait_send())
    for step in range(1, tensors):
        sums_copy(lax.rem(tpos + step, tensors)).wait_send()


def body(frames, tensors, q_proj, k_proj, v_proj, gain_q, gain_k, tiles):
    rows, width = q_proj.shape
    heads = width // HD
    vmem = pl.BlockSpec(memory_space=pltpu.VMEM)
    slots = -(-tiles.shape[1] // 8) * 8
    return pl.pallas_call(
        functools.partial(kernel, frames, tensors),
        out_shape=jax.ShapeDtypeStruct((rows, width), jnp.bfloat16),
        in_specs=[pl.BlockSpec(memory_space=pltpu.SMEM)] + [vmem] * 5,
        out_specs=vmem,
        scratch_shapes=[
            pltpu.VMEM((frames, rows, width), jnp.bfloat16),
            pltpu.VMEM((frames, rows, width), jnp.bfloat16),
            pltpu.VMEM((rows, width), jnp.bfloat16),
            pltpu.VMEM((tensors, 8, rows), jnp.float32),
            pltpu.VMEM((slots, rows), jnp.int32),
            pltpu.VMEM((heads, HD, rows), jnp.float32),
            pltpu.VMEM((8, rows), jnp.float32),
            pltpu.VMEM((8, rows), jnp.float32),
            pltpu.SemaphoreType.DMA((frames,)),
            pltpu.SemaphoreType.DMA((frames,)),
            pltpu.SemaphoreType.DMA((frames,)),
            pltpu.SemaphoreType.DMA((frames,)),
            pltpu.SemaphoreType.DMA((tensors,)),
            pltpu.SemaphoreType.DMA((tensors,)),
        ],
        compiler_params=pltpu.CompilerParams(
            collective_id=0, has_side_effects=True, vmem_limit_bytes=40 * 1024 * 1024
        ),
    )(tiles, q_proj, k_proj, v_proj, gain_q.reshape(1, width), gain_k.reshape(1, width))


def solution(mesh):
    return jax.shard_map(
        functools.partial(body, mesh.shape["frame"], mesh.shape["tensor"]),
        mesh=mesh,
        in_specs=(
            P(("dp", "frame"), "tensor"),
            P(("dp", "frame"), "tensor"),
            P(("dp", "frame"), "tensor"),
            P("tensor"),
            P("tensor"),
            P("dp", None),
        ),
        out_specs=P(("dp", "frame"), "tensor"),
        check_vma=False,
    )
```

time: 241 us -> 77.1 us (0.32); the launches traced: 237 us -> 76.4 us
  waiting for transfers between devices: 98.3 us -> 0 us
  Pallas kernels: 0 us -> 71.2 us
  local copies, waits for them, and re-layouts: 64.5 us -> 5.21 us
  matrix products: 43.3 us -> 0 us
  between operations: 13.5 us -> 0.01 us
  other arithmetic: 12.1 us -> 0 us
  blocking collectives: 4.94 us -> 0 us
    all_gather x1 -> x0, waiting for transfers between devices: 98.3 us -> none  [body(): portion = lax.all_gather(kv_pair, 'frame', axis=1, tiled=True)]
    pallas_call x0 -> x1, Pallas kernels: none -> 71.2 us  [body(): pl.pallas_call(functools.partial(kernel, frames, tensors), out_shape=jax....]
    dot_general x16 -> x0, matrix products: 43.3 us -> none  [the longest x8 27.6 us: attend(): jnp.einsum('hqk,khd->hqd', weights.astype(jnp.bfloat16), v_heads, preferr...]
    dynamic_slice x33 -> x0, local copies, waits for them, and re-layouts: 38.5 us -> none  [the longest x32 38.4 us: sweep(): final_state, unused = lax.scan(one_step, state_now, inputs)]
    broadcast_in_dim x8 -> x0, local copies, waits for them, and re-layouts: 12.8 us -> none  [attend(): listed = jnp.repeat(listed, tok_rows // q_tiles.shape[0], axis=0)[None]]
    reduce_sum x10 -> x0, other arithmetic: 7.71 us -> none  [the longest x8 6.45 us: attend(): new_sum = run_sum * factor + jnp.sum(weights, axis=-1)]
    slice x1 -> x0, local copies, waits for them, and re-layouts: 6.13 us -> none  [body(): portion[1]]
    psum x1 -> x0, blocking collectives: 4.94 us -> none  [body(): lax.psum((jnp.sum(q_wide * q_wide, axis=1), jnp.sum(k_wide * k_wide, axis...]
  transfers between devices with their start and end apart: 1 -> 0, of which waited for: 1 -> 0; matrix products, arithmetic and copies ran while one was open for 0% -> 0% of each run, Pallas kernels for 0% -> 0%
where the time goes in v1:
time: 77.1 us; the launch traced here: 76.4 us
  Pallas kernels  71.2 us (92%)
  local copies, waits for them, and re-layouts  5.21 us (7%)
    pallas_call x1, Pallas kernels, body(): pl.pallas_call(functools.partial(kernel, frames, tensors), out_shape=jax....  71.2 us
    unnamed x10, local copies, waits for them, and re-layouts  4.51 us

profile of v1, /device:TPU:4, one launch (start us, length us, event | category | flops | bytes accessed | tf_op | source)
XLA Modules:
  0.0 76.4 jit_solution(6402243498847281262)
XLA Ops:
  0.0 0.0 copy-start.3
  0.0 0.7 reshape.6.gq_ref
  0.7 0.0 copy-done.3
  0.7 0.8 %copy.7.tiles_ref = s32[32,12]{1,0:T(8,128)S(1)} copy(s32[32,12]{0,1:T(8,128)} %param.11) | data formatting | bytes 3072 | tf_op args[5]
  1.5 0.0 copy-start
  1.5 1.0 %copy-done = bf16[512,384]{1,0:T(8,128)(2,1)S(1)} copy-done((bf16[512,384]{1,0:T(8,128)(2,1)S(1)}, bf16[512,384]{1,0:T(8,128)(2,1)}, u32[]{:S(2)}) %copy-start) | copy-done | bytes 393240
  2.5 0.0 copy-start.1
  2.5 1.0 %copy-done.1 = bf16[512,384]{1,0:T(8,128)(2,1)S(1)} copy-done((bf16[512,384]{1,0:T(8,128)(2,1)S(1)}, bf16[512,384]{1,0:T(8,128)(2,1)}, u32[]{:S(2)}) %copy-start.1) | copy-done | bytes 393240
  3.5 0.0 copy-start.2
  3.5 1.0 %copy-done.2 = bf16[512,384]{1,0:T(8,128)(2,1)S(1)} copy-done((bf16[512,384]{1,0:T(8,128)(2,1)S(1)}, bf16[512,384]{1,0:T(8,128)(2,1)}, u32[]{:S(2)}) %copy-start.2) | copy-done | bytes 393240
  4.5 71.2 %shard_map.64 = bf16[512,384]{1,0:T(8,128)(2,1)S(1)} custom-call(s32[32,12]{1,0:T(8,128)S(1)} %copy.7.tiles_ref, bf16[512,384]{1,0:T(8,128)(2,1)S(1)} %copy-done, bf16[512,384]{1,0:T(8,128)(2,1)S(1)} %copy-done.1, bf16[512,384]{1,0:T(8,128)(2,1)S(1)} %copy-done.2, f32[1,384]{1,0:T(1,128)S(1)} %reshape.6.gq_ref, f32[1,384]{1,0:T(1,128)S(1)} %reshape.7.gk_ref), custom_call_target="tpu_custom_call" | custom-call | tf_op jit(solution)/shard_map/pallas_call | solution.py:239
  75.6 0.7 copy.9
  (1 shorter events, 0.0 us)
Async XLA Ops:
  0.0 0.7 copy-start.3
  1.5 1.0 %copy-start = (bf16[512,384]{1,0:T(8,128)(2,1)S(1)}, bf16[512,384]{1,0:T(8,128)(2,1)}, u32[]{:S(2)}) copy-start(bf16[512,384]{1,0:T(8,128)(2,1)} %q_ref.1) | copy-start | bytes 1179652
  2.5 1.0 %copy-start.1 = (bf16[512,384]{1,0:T(8,128)(2,1)S(1)}, bf16[512,384]{1,0:T(8,128)(2,1)}, u32[]{:S(2)}) copy-start(bf16[512,384]{1,0:T(8,128)(2,1)} %k_ref.1) | copy-start | bytes 1179652
  3.5 1.0 %copy-start.2 = (bf16[512,384]{1,0:T(8,128)(2,1)S(1)}, bf16[512,384]{1,0:T(8,128)(2,1)}, u32[]{:S(2)}) copy-start(bf16[512,384]{1,0:T(8,128)(2,1)} %v_ref.1) | copy-start | bytes 1179652

commit v2 on v1

--- a/solution.py
+++ b/solution.py
@@ -19,13 +19,18 @@
 def kernel(
     frames,
     tensors,
+    tiles_hbm,
+    q_hbm,
+    k_hbm,
+    v_hbm,
+    gq_hbm,
+    gk_hbm,
+    out_ref,
     tiles_ref,
     q_ref,
     k_ref,
-    v_ref,
     gq_ref,
     gk_ref,
-    out_ref,
     kbuf,
     vbuf,
     qn,
@@ -34,6 +39,7 @@
     acc_ref,
     max_ref,
     sum_ref,
+    load_sem,
     send_k,
     send_v,
     recv_k,
@@ -47,56 +53,126 @@
     heads = width // HD
     blocks = rows // BLK
     slots = tiles_ref.shape[1]
+    half = rows // 2
+
+    loads = [
+        pltpu.make_async_copy(source, target, load_sem.at[index])
+        for index, (source, target) in enumerate(
+            (
+                (q_hbm, q_ref),
+                (k_hbm, k_ref),
+                (v_hbm, vbuf.at[me]),
+                (tiles_hbm, tiles_ref),
+                (gq_hbm, gq_ref),
+                (gk_hbm, gk_ref),
+            )
+        )
+    ]
+    for load in loads:
+        load.start()
+
+    side = 1 - 2 * lax.rem(me, 2)
+    partner = me + side
+    ahead = me + 2 * side
+    behind = me - 2 * side
+
+    def inside(index):
+        return jnp.logical_and(index >= 0, index < frames)
 
     barrier = pltpu.get_barrier_semaphore()
-    for step in range(1, frames):
-        pl.semaphore_signal(
-            barrier, inc=1, device_id={"frame": lax.rem(me + step, frames)}, device_id_type=MESH
-        )
+    pl.semaphore_signal(barrier, inc=1, device_id={"frame": partner}, device_id_type=MESH)
+    for other in (me + 2, me - 2):
+
+        @pl.when(inside(other))
+        def _():
+            pl.semaphore_signal(barrier, inc=1, device_id={"frame": other}, device_id_type=MESH)
+
     for step in range(1, tensors):
         pl.semaphore_signal(
             barrier, inc=1, device_id={"tensor": lax.rem(tpos + step, tensors)}, device_id_type=MESH
         )
-    pl.semaphore_wait(barrier, frames - 1 + tensors - 1)
-
-    def full_copy(src, buf, send, recv, dest):
+    neighbours = inside(me + 2).astype(jnp.int32) + inside(me - 2).astype(jnp.int32)
+    pl.semaphore_wait(barrier, neighbours + tensors)
+
+    HEAD, FRONT, BACK = (0, BLK), (0, half), (half, rows - half)
+    ACROSS, UP, DOWN = 0, 1, 2
+    channels = {
+        "k": (kbuf, kbuf.at[me], send_k, recv_k),
+        "v": (vbuf, v_hbm, send_v, recv_v),
+    }
+
+    def copy(kind, origin, piece, dest, way, own=False):
+        buf, own_ref, send, recv = channels[kind]
+        part = int(piece is BACK)
+        window = pl.ds(piece[0], piece[1])
         return pltpu.make_async_remote_copy(
-            src_ref=src,
-            dst_ref=buf.at[me],
-            send_sem=send.at[dest],
-            recv_sem=recv.at[me],
+            src_ref=own_ref.at[window] if own else buf.at[origin, window],
+            dst_ref=buf.at[origin, window],
+            send_sem=send.at[way, part, origin],
+            recv_sem=recv.at[part, origin],
             device_id={"frame": dest},
             device_id_type=MESH,
         )
 
-    def first_copy(src, buf, send, recv, dest):
-        return pltpu.make_async_remote_copy(
-            src_ref=src.at[pl.ds(0, BLK)],
-            dst_ref=buf.at[me, pl.ds(0, BLK)],
-            send_sem=send.at[dest],
-            recv_sem=recv.at[me],
-            device_id={"frame": dest},
-            device_id_type=MESH,
-        )
-
-    side = 1 - 2 * lax.rem(me, 2)
-    order = (me + side, me + 2, me - 2, me - side)
-
-    def each_near(action):
-        for other in order:
-
-            @pl.when(jnp.logical_and(other >= 0, other < frames))
+    def arrived(kind, origin, piece):
+        buf, _, _, recv = channels[kind]
+        view = buf.at[origin, pl.ds(piece[0], piece[1])]
+        pltpu.make_async_copy(view, view, recv.at[int(piece is BACK), origin]).wait()
+
+    def own_sends(kind, act):
+        for first, second in ((FRONT, BACK), (BACK, FRONT)):
+            act(copy(kind, me, second, partner, ACROSS, own=True))
+            for other, way in ((me + 2, UP), (me - 2, DOWN)):
+
+                @pl.when(inside(other))
+                def _():
+                    act(copy(kind, me, first, other, way, own=True))
+
+    def near_relays(kind, act, wait):
+        if wait:
+            arrived(kind, partner, BACK)
+
+        @pl.when(inside(ahead))
+        def _():
+            act(copy(kind, partner, BACK, ahead, UP))
+            if wait:
+                arrived(kind, ahead, FRONT)
+            act(copy(kind, ahead, FRONT, partner, ACROSS))
+
+        @pl.when(inside(behind))
+        def _():
+            if wait:
+                arrived(kind, behind, FRONT)
+            act(copy(kind, behind, HEAD, partner, ACROSS))
+
+        @pl.when(jnp.logical_and(inside(ahead), inside(behind)))
+        def _():
+            act(copy(kind, ahead, HEAD, behind, DOWN))
+            act(copy(kind, behind, HEAD, ahead, UP))
+
+    def far_relays(kind, hops, act, wait):
+        for sign, way in ((1, DOWN), (-1, UP)):
+            origin = me + 2 * hops * sign
+            dest = me - 2 * sign
+
+            @pl.when(inside(origin))
             def _():
-                action(other)
-
-    def each_far(action):
-        @pl.loop(0, frames)
-        def _(other):
-            @pl.when(jnp.abs(other - me) > NEAR)
-            def _():
-                action(other)
-
-    each_near(lambda dest: full_copy(v_ref, vbuf, send_v, recv_v, dest).start())
+                if wait:
+                    arrived(kind, origin, HEAD)
+
+                @pl.when(inside(dest))
+                def _():
+                    act(copy(kind, origin, HEAD, dest, way))
+
+                act(copy(kind, origin, HEAD, partner, ACROSS))
+
+    def start(descriptor):
+        descriptor.start()
+
+    def finish(descriptor):
+        descriptor.wait_send()
+
+    own_sends("v", start)
 
     def squares(ref):
         total = None
@@ -105,6 +181,8 @@
             total = wide * wide if total is None else total + wide * wide
         return jnp.sum(jnp.transpose(total), axis=0, keepdims=True)
 
+    loads[0].wait()
+    loads[1].wait()
     sums[tpos] = jnp.concatenate(
         [squares(q_ref), squares(k_ref), jnp.zeros((6, rows), jnp.float32)], axis=0
     )
@@ -122,8 +200,8 @@
     for step in range(1, tensors):
         sums_copy(lax.rem(tpos + step, tensors)).start()
 
-    each_far(lambda dest: first_copy(v_ref, vbuf, send_v, recv_v, dest).start())
-
+    for load in loads[2:]:
+        load.wait()
     for slot in range(slots):
         listed[slot : slot + 1, :] = jnp.concatenate(
             [
@@ -154,10 +232,9 @@
     def store_q(columns, value):
         qn[:, columns] = value
 
-    normed(k_ref, 1, gk_ref, store_k)
-    each_near(lambda dest: full_copy(kbuf.at[me], kbuf, send_k, recv_k, dest).start())
-    each_far(lambda dest: first_copy(kbuf.at[me], kbuf, send_k, recv_k, dest).start())
-    normed(q_ref, 0, gq_ref, store_q)
+    normed(k_ref, 1, gk_ref[...].reshape(1, width), store_k)
+    own_sends("k", start)
+    normed(q_ref, 0, gq_ref[...].reshape(1, width), store_q)
 
     acc_ref[...] = jnp.zeros_like(acc_ref)
     max_ref[...] = jnp.full_like(max_ref, MASKED)
@@ -201,32 +278,62 @@
             )
             acc_ref[head] = acc_ref[head] * shrink + product
 
-    attend(me, kbuf.at[me], v_ref)
-
-    def near_step(other):
-        pltpu.make_async_copy(vbuf.at[other], vbuf.at[other], recv_v.at[other]).wait()
-        pltpu.make_async_copy(kbuf.at[other], kbuf.at[other], recv_k.at[other]).wait()
-        attend(other, kbuf.at[other], vbuf.at[other])
-
-    each_near(near_step)
-
-    def far_step(other):
-        piece_v = vbuf.at[other, pl.ds(0, BLK)]
-        piece_k = kbuf.at[other, pl.ds(0, BLK)]
-        pltpu.make_async_copy(piece_v, piece_v, recv_v.at[other]).wait()
-        pltpu.make_async_copy(piece_k, piece_k, recv_k.at[other]).wait()
-        attend(other, piece_k, piece_v)
-
-    each_far(far_step)
+    last_hop = (frames - 1) // 2
+    near_relays("v", start, True)
+    attend(me, kbuf.at[me], vbuf.at[me])
+    for hops in range(2, last_hop + 1):
+        far_relays("v", hops, start, True)
+    near_relays("k", start, True)
+
+    arrived("v", partner, FRONT)
+    arrived("k", partner, FRONT)
+    attend(partner, kbuf.at[partner], vbuf.at[partner])
+
+    def neighbour_step(other):
+        @pl.when(inside(other))
+        def _():
+            arrived("v", other, BACK)
+            arrived("k", other, BACK)
+            attend(other, kbuf.at[other], vbuf.at[other])
+
+    for hops in range(2, last_hop + 1):
+        far_relays("k", hops, start, True)
+    neighbour_step(ahead)
+    neighbour_step(behind)
+
+    @pl.loop(0, frames)
+    def _(other):
+        distance = jnp.abs(other - me)
+        same_lane = lax.rem(distance, 2) == 0
+
+        @pl.when(distance > NEAR)
+        def _():
+            @pl.when(jnp.logical_not(same_lane))
+            def _():
+                arrived("v", other, HEAD)
+                arrived("k", other, HEAD)
+
+            attend(other, kbuf.at[other, pl.ds(0, BLK)], vbuf.at[other, pl.ds(0, BLK)])
+
+    diagonal = me - side
+
+    @pl.when(inside(diagonal))
+    def _():
+        arrived("v", diagonal, FRONT)
+        arrived("v", diagonal, BACK)
+        arrived("k", diagonal, FRONT)
+        arrived("k", diagonal, BACK)
+        attend(diagonal, kbuf.at[diagonal], vbuf.at[diagonal])
 
     for head in range(heads):
         value = acc_ref[head] / sum_ref[head : head + 1, :]
         out_ref[:, head * HD : (head + 1) * HD] = jnp.transpose(value).astype(jnp.bfloat16)
 
-    each_near(lambda dest: full_copy(v_ref, vbuf, send_v, recv_v, dest).wait_send())
-    each_near(lambda dest: full_copy(kbuf.at[me], kbuf, send_k, recv_k, dest).wait_send())
-    each_far(lambda dest: first_copy(v_ref, vbuf, send_v, recv_v, dest).wait_send())
-    each_far(lambda dest: first_copy(kbuf.at[me], kbuf, send_k, recv_k, dest).wait_send())
+    for kind in ("v", "k"):
+        own_sends(kind, finish)
+        near_relays(kind, finish, False)
+        for hops in range(2, last_hop + 1):
+            far_relays(kind, hops, finish, False)
     for step in range(1, tensors):
         sums_copy(lax.rem(tpos + step, tensors)).wait_send()
 
@@ -239,9 +346,14 @@
     return pl.pallas_call(
         functools.partial(kernel, frames, tensors),
         out_shape=jax.ShapeDtypeStruct((rows, width), jnp.bfloat16),
-        in_specs=[pl.BlockSpec(memory_space=pltpu.SMEM)] + [vmem] * 5,
+        in_specs=[pl.BlockSpec(memory_space=pltpu.HBM)] * 6,
         out_specs=vmem,
         scratch_shapes=[
+            pltpu.SMEM(tiles.shape, jnp.int32),
+            pltpu.VMEM((rows, width), jnp.bfloat16),
+            pltpu.VMEM((rows, width), jnp.bfloat16),
+            pltpu.VMEM((width,), jnp.float32),
+            pltpu.VMEM((width,), jnp.float32),
             pltpu.VMEM((frames, rows, width), jnp.bfloat16),
             pltpu.VMEM((frames, rows, width), jnp.bfloat16),
             pltpu.VMEM((rows, width), jnp.bfloat16),
@@ -250,17 +362,18 @@
             pltpu.VMEM((heads, HD, rows), jnp.float32),
             pltpu.VMEM((8, rows), jnp.float32),
             pltpu.VMEM((8, rows), jnp.float32),
-            pltpu.SemaphoreType.DMA((frames,)),
-            pltpu.SemaphoreType.DMA((frames,)),
-            pltpu.SemaphoreType.DMA((frames,)),
-            pltpu.SemaphoreType.DMA((frames,)),
+            pltpu.SemaphoreType.DMA((6,)),
+            pltpu.SemaphoreType.DMA((3, 2, frames)),
+            pltpu.SemaphoreType.DMA((3, 2, frames)),
+            pltpu.SemaphoreType.DMA((2, frames)),
+            pltpu.SemaphoreType.DMA((2, frames)),
             pltpu.SemaphoreType.DMA((tensors,)),
             pltpu.SemaphoreType.DMA((tensors,)),
         ],
         compiler_params=pltpu.CompilerParams(
             collective_id=0, has_side_effects=True, vmem_limit_bytes=40 * 1024 * 1024
         ),
-    )(tiles, q_proj, k_proj, v_proj, gain_q.reshape(1, width), gain_k.reshape(1, width))
+    )(tiles, q_proj, k_proj, v_proj, gain_q, gain_k)
 
 
 def solution(mesh):

time: 77.1 us -> 52.9 us (0.69)
  Pallas kernels: 71.2 us -> 48 us
    pallas_call x1, Pallas kernels: 71.2 us -> 48 us  [body(): pl.pallas_call(functools.partial(kernel, frames, tensors), out_shape=jax....]
    unnamed x10 -> x12, local copies, waits for them, and re-layouts: 4.51 us -> 4.54 us
where the time goes in v2:
time: 52.9 us; the launch traced here: 52.6 us
  Pallas kernels  48 us (91%)
  local copies, waits for them, and re-layouts  4.54 us (9%)
    pallas_call x1, Pallas kernels, body(): pl.pallas_call(functools.partial(kernel, frames, tensors), out_shape=jax....  48 us
    unnamed x12, local copies, waits for them, and re-layouts  4.54 us

profile of v2, /device:TPU:4, one launch (start us, length us, event | category | flops | bytes accessed | tf_op | source)
XLA Modules:
  0.0 52.6 jit_solution(9363569159936415987)
XLA Ops:
  0.0 0.0 copy-start.4
  0.0 0.0 copy-start.3
  0.0 0.8 %copy.7.tiles_hbm = s32[32,12]{1,0:T(8,128)S(1)} copy(s32[32,12]{0,1:T(8,128)} %param.11) | data formatting | bytes 3072 | tf_op args[5]
  0.8 0.0 copy-done.4
  0.8 0.0 copy-done.3
  0.8 0.0 copy-start
  0.8 1.0 %copy-done = bf16[512,384]{1,0:T(8,128)(2,1)S(1)} copy-done((bf16[512,384]{1,0:T(8,128)(2,1)S(1)}, bf16[512,384]{1,0:T(8,128)(2,1)}, u32[]{:S(2)}) %copy-start) | copy-done | bytes 393240
  1.8 0.0 copy-start.1
  1.8 1.0 %copy-done.1 = bf16[512,384]{1,0:T(8,128)(2,1)S(1)} copy-done((bf16[512,384]{1,0:T(8,128)(2,1)S(1)}, bf16[512,384]{1,0:T(8,128)(2,1)}, u32[]{:S(2)}) %copy-start.1) | copy-done | bytes 393240
  2.8 0.0 copy-start.2
  2.8 1.0 %copy-done.2 = bf16[512,384]{1,0:T(8,128)(2,1)S(1)} copy-done((bf16[512,384]{1,0:T(8,128)(2,1)S(1)}, bf16[512,384]{1,0:T(8,128)(2,1)}, u32[]{:S(2)}) %copy-start.2) | copy-done | bytes 393240
  3.8 48.0 %shard_map.64 = bf16[512,384]{1,0:T(8,128)(2,1)S(1)} custom-call(s32[32,12]{1,0:T(8,128)S(1)} %copy.7.tiles_hbm, bf16[512,384]{1,0:T(8,128)(2,1)S(1)} %copy-done, bf16[512,384]{1,0:T(8,128)(2,1)S(1)} %copy-done.1, bf16[512,384]{1,0:T(8,128)(2,1)S(1)} %copy-done.2, f32[384]{0:T(512)S(1)} %copy-done.3, f32[384]{0:T(512)S(1)} %copy-done.4), custom_call_target="tpu_custom_call" | custom-call | tf_op jit(solution)/shard_map/pallas_call | solution.py:346
  51.8 0.7 %copy.9 = bf16[512,384]{1,0:T(8,128)(2,1)} copy(bf16[512,384]{1,0:T(8,128)(2,1)S(1)} %shard_map.64) | data formatting | bytes 786432
Async XLA Ops:
  0.0 0.8 %copy-start.4 = (f32[384]{0:T(512)S(1)}, f32[384]{0:T(512)}, u32[]{:S(2)}) copy-start(f32[384]{0:T(512)} %gk_hbm.1) | copy-start | bytes 4612
  0.0 0.8 %copy-start.3 = (f32[384]{0:T(512)S(1)}, f32[384]{0:T(512)}, u32[]{:S(2)}) copy-start(f32[384]{0:T(512)} %gq_hbm.1) | copy-start | bytes 4612
  0.8 1.0 %copy-start = (bf16[512,384]{1,0:T(8,128)(2,1)S(1)}, bf16[512,384]{1,0:T(8,128)(2,1)}, u32[]{:S(2)}) copy-start(bf16[512,384]{1,0:T(8,128)(2,1)} %q_hbm.1) | copy-start | bytes 1179652
  1.8 1.0 %copy-start.1 = (bf16[512,384]{1,0:T(8,128)(2,1)S(1)}, bf16[512,384]{1,0:T(8,128)(2,1)}, u32[]{:S(2)}) copy-start(bf16[512,384]{1,0:T(8,128)(2,1)} %k_hbm.1) | copy-start | bytes 1179652
  2.8 1.0 %copy-start.2 = (bf16[512,384]{1,0:T(8,128)(2,1)S(1)}, bf16[512,384]{1,0:T(8,128)(2,1)}, u32[]{:S(2)}) copy-start(bf16[512,384]{1,0:T(8,128)(2,1)} %v_hbm.1) | copy-start | bytes 1179652

commit v3 on v2

--- a/solution.py
+++ b/solution.py
@@ -52,7 +52,7 @@
     rows, width = q_ref.shape
     heads = width // HD
     blocks = rows // BLK
-    slots = tiles_ref.shape[1]
+    slots = tiles_ref.shape[0]
     half = rows // 2
 
     loads = [
@@ -129,26 +129,35 @@
                     act(copy(kind, me, first, other, way, own=True))
 
     def near_relays(kind, act, wait):
+        @pl.when(inside(ahead))
+        def _():
+            if wait:
+                arrived(kind, ahead, FRONT)
+
+        @pl.when(inside(behind))
+        def _():
+            if wait:
+                arrived(kind, behind, FRONT)
+
+        @pl.when(jnp.logical_and(inside(ahead), inside(behind)))
+        def _():
+            act(copy(kind, ahead, HEAD, behind, DOWN))
+            act(copy(kind, behind, HEAD, ahead, UP))
+
+        @pl.when(inside(behind))
+        def _():
+            act(copy(kind, behind, HEAD, partner, ACROSS))
+
+        @pl.when(inside(ahead))
+        def _():
+            act(copy(kind, ahead, FRONT, partner, ACROSS))
+
         if wait:
             arrived(kind, partner, BACK)
 
         @pl.when(inside(ahead))
         def _():
             act(copy(kind, partner, BACK, ahead, UP))
-            if wait:
-                arrived(kind, ahead, FRONT)
-            act(copy(kind, ahead, FRONT, partner, ACROSS))
-
-        @pl.when(inside(behind))
-        def _():
-            if wait:
-                arrived(kind, behind, FRONT)
-            act(copy(kind, behind, HEAD, partner, ACROSS))
-
-        @pl.when(jnp.logical_and(inside(ahead), inside(behind)))
-        def _():
-            act(copy(kind, ahead, HEAD, behind, DOWN))
-            act(copy(kind, behind, HEAD, ahead, UP))
 
     def far_relays(kind, hops, act, wait):
         for sign, way in ((1, DOWN), (-1, UP)):
@@ -205,7 +214,7 @@
     for slot in range(slots):
         listed[slot : slot + 1, :] = jnp.concatenate(
             [
-                jnp.full((1, BLK), tiles_ref[me * blocks + block, slot], jnp.int32)
+                jnp.full((1, BLK), tiles_ref[slot, me * blocks + block], jnp.int32)
                 for block in range(blocks)
             ],
             axis=1,
@@ -241,11 +250,11 @@
     sum_ref[...] = jnp.zeros_like(sum_ref)
     to_exponent = math.log2(math.e) / math.sqrt(HD)
 
-    def attend(slab, keys, values):
+    def attend(slab, keys, values, first=0):
         count = keys.shape[0] // BLK
         biases = []
         for block in range(count):
-            hit = jnp.any(listed[0:slots, :] == slab * blocks + block, axis=0, keepdims=True)
+            hit = jnp.any(listed[0:slots, :] == slab * blocks + first + block, axis=0, keepdims=True)
             biases.append(jnp.where(hit, 0.0, MASKED))
         for head in range(heads):
             columns = slice(head * HD, (head + 1) * HD)
@@ -285,10 +294,6 @@
         far_relays("v", hops, start, True)
     near_relays("k", start, True)
 
-    arrived("v", partner, FRONT)
-    arrived("k", partner, FRONT)
-    attend(partner, kbuf.at[partner], vbuf.at[partner])
-
     def neighbour_step(other):
         @pl.when(inside(other))
         def _():
@@ -296,34 +301,55 @@
             arrived("k", other, BACK)
             attend(other, kbuf.at[other], vbuf.at[other])
 
+    def attend_head(other):
+        attend(other, kbuf.at[other, pl.ds(0, BLK)], vbuf.at[other, pl.ds(0, BLK)])
+
+    def partner_step():
+        arrived("v", partner, FRONT)
+        arrived("k", partner, FRONT)
+        attend(partner, kbuf.at[partner], vbuf.at[partner])
+
+    steps = [partner_step, lambda: neighbour_step(ahead), lambda: neighbour_step(behind)]
     for hops in range(2, last_hop + 1):
+        if steps:
+            steps.pop(0)()
         far_relays("k", hops, start, True)
-    neighbour_step(ahead)
-    neighbour_step(behind)
-
-    @pl.loop(0, frames)
-    def _(other):
-        distance = jnp.abs(other - me)
-        same_lane = lax.rem(distance, 2) == 0
-
-        @pl.when(distance > NEAR)
-        def _():
-            @pl.when(jnp.logical_not(same_lane))
+    for step in steps:
+        step()
+
+    @pl.loop(2, last_hop + 1)
+    def _(hops):
+        for origin in (me + 2 * hops, me - 2 * hops):
+
+            @pl.when(inside(origin))
             def _():
-                arrived("v", other, HEAD)
-                arrived("k", other, HEAD)
-
-            attend(other, kbuf.at[other, pl.ds(0, BLK)], vbuf.at[other, pl.ds(0, BLK)])
+                attend_head(origin)
 
     diagonal = me - side
 
     @pl.when(inside(diagonal))
     def _():
-        arrived("v", diagonal, FRONT)
-        arrived("v", diagonal, BACK)
-        arrived("k", diagonal, FRONT)
-        arrived("k", diagonal, BACK)
-        attend(diagonal, kbuf.at[diagonal], vbuf.at[diagonal])
+        for piece in (FRONT, BACK):
+            arrived("v", diagonal, piece)
+            arrived("k", diagonal, piece)
+            window = pl.ds(piece[0], piece[1])
+            attend(
+                diagonal,
+                kbuf.at[diagonal, window],
+                vbuf.at[diagonal, window],
+                piece[0] // BLK,
+            )
+
+    @pl.loop(1, frames // 2)
+    def _(index):
+        distance = 2 * index + 1
+        for origin in (me + distance, me - distance):
+
+            @pl.when(inside(origin))
+            def _():
+                arrived("v", origin, HEAD)
+                arrived("k", origin, HEAD)
+                attend_head(origin)
 
     for head in range(heads):
         value = acc_ref[head] / sum_ref[head : head + 1, :]
@@ -349,7 +375,7 @@
         in_specs=[pl.BlockSpec(memory_space=pltpu.HBM)] * 6,
         out_specs=vmem,
         scratch_shapes=[
-            pltpu.SMEM(tiles.shape, jnp.int32),
+            pltpu.SMEM(tiles.shape[::-1], jnp.int32),
             pltpu.VMEM((rows, width), jnp.bfloat16),
             pltpu.VMEM((rows, width), jnp.bfloat16),
             pltpu.VMEM((width,), jnp.float32),
@@ -371,9 +397,9 @@
             pltpu.SemaphoreType.DMA((tensors,)),
         ],
         compiler_params=pltpu.CompilerParams(
-            collective_id=0, has_side_effects=True, vmem_limit_bytes=40 * 1024 * 1024
+            collective_id=0, has_side_effects=True, vmem_limit_bytes=63 * 1024 * 1024
         ),
-    )(tiles, q_proj, k_proj, v_proj, gain_q, gain_k)
+    )(tiles.T, q_proj, k_proj, v_proj, gain_q, gain_k)
 
 
 def solution(mesh):

time: 52.9 us -> 49.5 us (0.936)
  local copies, waits for them, and re-layouts: 4.54 us -> 1.78 us
    unnamed x12 -> x1, local copies, waits for them, and re-layouts: 4.54 us -> 1.78 us
where the time goes in v3:
time: 49.5 us; the launch traced here: 49.4 us
  Pallas kernels  47.6 us (96%)
  local copies, waits for them, and re-layouts  1.78 us (4%)
    pallas_call x1, Pallas kernels, body(): pl.pallas_call(functools.partial(kernel, frames, tensors), out_shape=jax....  47.6 us
    unnamed x1, local copies, waits for them, and re-layouts  1.78 us

profile of v3, /device:TPU:4, one launch (start us, length us, event | category | flops | bytes accessed | tf_op | source)
XLA Modules:
  0.0 49.4 jit_solution(9010099466763867997)
XLA Ops:
  0.0 47.6 %shard_map.64 = bf16[512,384]{1,0:T(8,128)(2,1)} custom-call(s32[12,32]{1,0:T(8,128)} %bitcast.1, bf16[512,384]{1,0:T(8,128)(2,1)} %q_hbm.1, bf16[512,384]{1,0:T(8,128)(2,1)} %k_hbm.1, bf16[512,384]{1,0:T(8,128)(2,1)} %v_hbm.1, f32[384]{0:T(512)} %gq_hbm.1, f32[384]{0:T(512)} %gk_hbm.1), custom_call_target="tpu_custom_call" | custom-call | tf_op jit(solution)/shard_map/pallas_call | solution.py:372
  47.6 1.8 %copy.8 = bf16[512,384]{1,0:T(8,128)(2,1)} copy(bf16[512,384]{1,0:T(8,128)(2,1)} %shard_map.64) | data formatting | bytes 786432

commit v4 on v3

--- a/solution.py
+++ b/solution.py
@@ -128,7 +128,7 @@
                 def _():
                     act(copy(kind, me, first, other, way, own=True))
 
-    def near_relays(kind, act, wait):
+    def head_relays(kind, act, wait):
         @pl.when(inside(ahead))
         def _():
             if wait:
@@ -148,15 +148,10 @@
         def _():
             act(copy(kind, behind, HEAD, partner, ACROSS))
 
+    def diagonal_relays(kind, act):
         @pl.when(inside(ahead))
         def _():
             act(copy(kind, ahead, FRONT, partner, ACROSS))
-
-        if wait:
-            arrived(kind, partner, BACK)
-
-        @pl.when(inside(ahead))
-        def _():
             act(copy(kind, partner, BACK, ahead, UP))
 
     def far_relays(kind, hops, act, wait):
@@ -288,11 +283,9 @@
             acc_ref[head] = acc_ref[head] * shrink + product
 
     last_hop = (frames - 1) // 2
-    near_relays("v", start, True)
+    head_relays("v", start, True)
     attend(me, kbuf.at[me], vbuf.at[me])
-    for hops in range(2, last_hop + 1):
-        far_relays("v", hops, start, True)
-    near_relays("k", start, True)
+    head_relays("k", start, True)
 
     def neighbour_step(other):
         @pl.when(inside(other))
@@ -305,17 +298,22 @@
         attend(other, kbuf.at[other, pl.ds(0, BLK)], vbuf.at[other, pl.ds(0, BLK)])
 
     def partner_step():
-        arrived("v", partner, FRONT)
-        arrived("k", partner, FRONT)
+        for piece in (BACK, FRONT):
+            arrived("v", partner, piece)
+            arrived("k", partner, piece)
         attend(partner, kbuf.at[partner], vbuf.at[partner])
 
-    steps = [partner_step, lambda: neighbour_step(ahead), lambda: neighbour_step(behind)]
-    for hops in range(2, last_hop + 1):
-        if steps:
-            steps.pop(0)()
+    partner_step()
+    diagonal_relays("v", start)
+    if last_hop >= 2:
+        far_relays("v", 2, start, True)
+        far_relays("k", 2, start, True)
+    diagonal_relays("k", start)
+    neighbour_step(ahead)
+    neighbour_step(behind)
+    for hops in range(3, last_hop + 1):
+        far_relays("v", hops, start, True)
         far_relays("k", hops, start, True)
-    for step in steps:
-        step()
 
     @pl.loop(2, last_hop + 1)
     def _(hops):
@@ -323,6 +321,17 @@
 
             @pl.when(inside(origin))
             def _():
+                attend_head(origin)
+
+    @pl.loop(1, frames // 2)
+    def _(index):
+        distance = 2 * index + 1
+        for origin in (me + distance, me - distance):
+
+            @pl.when(inside(origin))
+            def _():
+                arrived("v", origin, HEAD)
+                arrived("k", origin, HEAD)
                 attend_head(origin)
 
     diagonal = me - side
@@ -340,24 +349,14 @@
                 piece[0] // BLK,
             )
 
-    @pl.loop(1, frames // 2)
-    def _(index):
-        distance = 2 * index + 1
-        for origin in (me + distance, me - distance):
-
-            @pl.when(inside(origin))
-            def _():
-                arrived("v", origin, HEAD)
-                arrived("k", origin, HEAD)
-                attend_head(origin)
-
     for head in range(heads):
         value = acc_ref[head] / sum_ref[head : head + 1, :]
         out_ref[:, head * HD : (head + 1) * HD] = jnp.transpose(value).astype(jnp.bfloat16)
 
     for kind in ("v", "k"):
         own_sends(kind, finish)
-        near_relays(kind, finish, False)
+        head_relays(kind, finish, False)
+        diagonal_relays(kind, finish)
         for hops in range(2, last_hop + 1):
             far_relays(kind, hops, finish, False)
     for step in range(1, tensors):

time: 49.5 us -> 46.9 us (0.947)
  Pallas kernels: 47.6 us -> 44.9 us
    pallas_call x1, Pallas kernels: 47.6 us -> 44.9 us  [body(): pl.pallas_call(functools.partial(kernel, frames, tensors), out_shape=jax....]
where the time goes in v4:
time: 46.9 us; the launch traced here: 46.7 us
  Pallas kernels  44.9 us (96%)
  local copies, waits for them, and re-layouts  1.78 us (4%)
    pallas_call x1, Pallas kernels, body(): pl.pallas_call(functools.partial(kernel, frames, tensors), out_shape=jax....  44.9 us
    unnamed x1, local copies, waits for them, and re-layouts  1.78 us

profile of v4, /device:TPU:4, one launch (start us, length us, event | category | flops | bytes accessed | tf_op | source)
XLA Modules:
  0.0 46.7 jit_solution(452795701301480783)
XLA Ops:
  0.0 44.9 %shard_map.64 = bf16[512,384]{1,0:T(8,128)(2,1)} custom-call(s32[12,32]{1,0:T(8,128)} %bitcast.1, bf16[512,384]{1,0:T(8,128)(2,1)} %q_hbm.1, bf16[512,384]{1,0:T(8,128)(2,1)} %k_hbm.1, bf16[512,384]{1,0:T(8,128)(2,1)} %v_hbm.1, f32[384]{0:T(512)} %gq_hbm.1, f32[384]{0:T(512)} %gk_hbm.1), custom_call_target="tpu_custom_call" | custom-call | tf_op jit(solution)/shard_map/pallas_call | solution.py:371
  44.9 1.8 %copy.8 = bf16[512,384]{1,0:T(8,128)(2,1)} copy(bf16[512,384]{1,0:T(8,128)(2,1)} %shard_map.64) | data formatting | bytes 786432
